TPU v7x, 128 devices: a whole 4x4x4 slice. The times are simulated.
128 devices in a mesh: tower: 2 (over z_hi), seq: 8 (over x, core), rep: 8 (over y, z_lo).
Axes of the slice: x: 4, y: 4, z: 4 (z_hi: 2, z_lo: 2; z = z_hi * 2 + z_lo), core: 2. Of those that a mesh axis runs over, the one named last changes fastest.
Arguments:
- queries: bfloat16 [2, 3072, 3072], P('tower', 'seq', 'rep'), may hold values from -8.1 to 8.1
- key_input: bfloat16 [2, 3072, 3072], P('tower', 'seq', 'rep'), may hold values from -8.1 to 8.1
- values: bfloat16 [2, 3072, 3072], P('tower', 'seq', 'rep'), may hold values from -6 to 6
- cotangent: bfloat16 [2, 3072, 3072], P('tower', 'seq', 'rep'), may hold values from -6 to 6
- positions: int32 [2, 3072], P('tower', 'seq'), may hold values from 0 to 1023
- lengths: int32 [2, 8], P('tower', 'seq'), may hold values from 2 to 384, as said below
Outputs:
- attended: bfloat16 [2, 3072, 3072], P('tower', 'seq', 'rep')
- grad_query: bfloat16 [2, 3072, 3072], P('tower', 'seq', 'rep')
- grad_key: bfloat16 [2, 3072, 3072], P('tower', 'seq', 'rep')
- grad_value: bfloat16 [2, 3072, 3072], P('tower', 'seq', 'rep')
Inputs may be any that keep to these rules, and one draw needn't show every extreme that they name: In each block of 384 slots the first lengths slots hold tokens and the rest are padding.
All inputs are finite; a program needn't handle non-finite values.
Results may differ from a plain program's by a relative error of at most 0.012.
The roundings to bfloat16 on the way count: a program that leaves them out, or rounds other values in their place, can miss the bound.
Values may be sent and summed in bfloat16 or wider, within the bound.
A program may use at most 128 MiB of HBM per device.

v0:
```python
import math

import jax
import jax.numpy as jnp
from jax import lax
from jax.sharding import PartitionSpec as P

HEAD_DIM = 128


def phases(positions, width):
    half_width = width // 2
    rates = jnp.exp(-math.log(10000.0) * jnp.arange(half_width, dtype=jnp.float32) / half_width)
    angles = positions.astype(jnp.float32)[..., None] * rates
    return (jnp.cos(angles)[..., None, :], jnp.sin(angles)[..., None, :])


def rotate(tensor, cosine_table, sine_table):
    half_width = tensor.shape[-1] // 2
    leading = tensor[..., :half_width]
    trailing = tensor[..., half_width:]
    return jnp.concatenate(
        [
            leading * cosine_table - trailing * sine_table,
            trailing * cosine_table + leading * sine_table,
        ],
        axis=-1,
    )


def unrotate(tensor, cosine_table, sine_table):
    half_width = tensor.shape[-1] // 2
    leading = tensor[..., :half_width]
    trailing = tensor[..., half_width:]
    return jnp.concatenate(
        [
            leading * cosine_table + trailing * sine_table,
            trailing * cosine_table - leading * sine_table,
        ],
        axis=-1,
    )


def branch(query_rows, grad_rows, key_rows, value_rows, key_valid, scaling):
    scores = jnp.dot(query_rows, key_rows.T, preferred_element_type=jnp.float32) * scaling
    scores = jnp.where(key_valid[None, :], scores, -jnp.inf)
    largest = jnp.max(scores, axis=1, keepdims=True)
    log_total = largest + jnp.log(jnp.sum(jnp.exp(scores - largest), axis=1, keepdims=True))
    probabilities = jnp.exp(scores - log_total).astype(jnp.bfloat16)
    branch_out = jnp.dot(probabilities, value_rows, preferred_element_type=jnp.float32)
    row_dot = jnp.sum(grad_rows.astype(jnp.float32) * branch_out, axis=1, keepdims=True)
    value_grad = jnp.dot(probabilities.T, grad_rows, preferred_element_type=jnp.float32)
    prob_grad = jnp.dot(grad_rows, value_rows.T, preferred_element_type=jnp.float32)
    score_grad = (probabilities.astype(jnp.float32) * (prob_grad - row_dot) * scaling).astype(
        jnp.bfloat16
    )
    query_grad = jnp.dot(score_grad, key_rows, preferred_element_type=jnp.float32)
    key_grad = jnp.dot(score_grad.T, query_rows, preferred_element_type=jnp.float32)
    return (branch_out, query_grad, key_grad, value_grad, log_total, row_dot)


def body(queries, key_input, values, cotangent, positions, lengths):
    slot_count = queries.shape[1]
    head_count = queries.shape[2] // HEAD_DIM
    shaped = (slot_count, head_count, HEAD_DIM)
    cosine_table, sine_table = phases(positions[0], HEAD_DIM)
    rot_queries = rotate(
        queries[0].reshape(shaped).astype(jnp.float32), cosine_table, sine_table
    ).astype(jnp.bfloat16)
    rot_keys = rotate(
        key_input[0].reshape(shaped).astype(jnp.float32), cosine_table, sine_table
    ).astype(jnp.bfloat16)
    value_heads = values[0].reshape(shaped)
    present = jnp.arange(slot_count, dtype=jnp.int32) < lengths[0, 0]
    grad_heads = jnp.where(
        present[:, None, None], cotangent[0].reshape(shaped), jnp.zeros((), jnp.bfloat16)
    )
    length_table = lax.all_gather(lengths.reshape(1), ("tower", "seq"), axis=0, tiled=True)
    key_valid = (
        jnp.arange(slot_count, dtype=jnp.int32)[None, None, :]
        < length_table.reshape(2, -1)[..., None]
    ).reshape(2, -1)
    joined_keys, joined_values = (
        lax.all_gather(rot_keys, ("tower", "seq"), axis=0, tiled=True),
        lax.all_gather(value_heads, ("tower", "seq"), axis=0, tiled=True),
    )
    key_heads = joined_keys.reshape(2, -1, head_count, HEAD_DIM)
    val_heads = joined_values.reshape(2, -1, head_count, HEAD_DIM)
    scaling = 1.0 / math.sqrt(HEAD_DIM)

    def per_head(head_index, carry):
        merged_out, merged_qgrad, merged_kgrad, merged_vgrad, stats_total, stats_dot = carry
        query_rows = lax.dynamic_index_in_dim(rot_queries, head_index, 1, keepdims=False)
        grad_rows = lax.dynamic_index_in_dim(grad_heads, head_index, 1, keepdims=False)
        key_rows = lax.dynamic_index_in_dim(key_heads, head_index, 2, keepdims=False)
        value_rows = lax.dynamic_index_in_dim(val_heads, head_index, 2, keepdims=False)
        out_video, qgrad_video, kgrad_video, vgrad_video, total_video, dot_video = branch(
            query_rows, grad_rows, key_rows[0], value_rows[0], key_valid[0], scaling
        )
        out_audio, qgrad_audio, kgrad_audio, vgrad_audio, total_audio, dot_audio = branch(
            query_rows, grad_rows, key_rows[1], value_rows[1], key_valid[1], scaling
        )
        key_stack = jnp.concatenate([kgrad_video, kgrad_audio], axis=0)
        value_stack = jnp.concatenate([vgrad_video, vgrad_audio], axis=0)
        key_total, value_total = (
            lax.psum_scatter(key_stack, ("tower", "seq"), scatter_dimension=0, tiled=True),
            lax.psum_scatter(value_stack, ("tower", "seq"), scatter_dimension=0, tiled=True),
        )
        merged_kgrad = lax.dynamic_update_index_in_dim(
            merged_kgrad, key_total.astype(jnp.bfloat16), head_index, 1
        )
        merged_vgrad = lax.dynamic_update_index_in_dim(
            merged_vgrad, value_total.astype(jnp.bfloat16), head_index, 1
        )
        merged_out = lax.dynamic_update_index_in_dim(
            merged_out, (out_video + out_audio).astype(jnp.bfloat16), head_index, 1
        )
        merged_qgrad = lax.dynamic_update_index_in_dim(
            merged_qgrad, (qgrad_video + qgrad_audio).astype(jnp.bfloat16), head_index, 1
        )
        return (merged_out, merged_qgrad, merged_kgrad, merged_vgrad, stats_total, stats_dot)

    empty = jnp.zeros(shaped, jnp.bfloat16)
    empty_stats = jnp.zeros((slot_count, 2, head_count), jnp.float32)
    merged_out, merged_qgrad, merged_kgrad, merged_vgrad, stats_total, stats_dot = lax.fori_loop(
        0, head_count, per_head, (empty, empty, empty, empty, empty_stats, empty_stats)
    )
    attended = jnp.where(present[:, None, None], merged_out, jnp.zeros((), jnp.bfloat16)).reshape(
        1, slot_count, -1
    )
    grad_query = (
        unrotate(merged_qgrad.astype(jnp.float32), cosine_table, sine_table)
        .astype(jnp.bfloat16)
        .reshape(1, slot_count, -1)
    )
    grad_key = (
        unrotate(merged_kgrad.astype(jnp.float32), cosine_table, sine_table)
        .astype(jnp.bfloat16)
        .reshape(1, slot_count, -1)
    )
    grad_value = merged_vgrad.reshape(1, slot_count, -1)
    return (attended, grad_query, grad_key, grad_value)


def solution(mesh):
    return jax.shard_map(
        body,
        mesh=mesh,
        in_specs=(
            P("tower", "seq", "rep"),
            P("tower", "seq", "rep"),
            P("tower", "seq", "rep"),
            P("tower", "seq", "rep"),
            P("tower", "seq"),
            P("tower", "seq"),
        ),
        out_specs=(
            P("tower", "seq", "rep"),
            P("tower", "seq", "rep"),
            P("tower", "seq", "rep"),
            P("tower", "seq", "rep"),
        ),
        check_vma=False,
    )
```

profile of v0, /device:TPU:0, one launch (start us, length us, event | category | flops | bytes accessed | tf_op | source)
XLA Modules:
  0.0 696.9 jit_solution(2209201979635282674)
XLA Ops:
  15.5 14.8 %all-reduce = s32[16]{0:T(128)S(1)} all-reduce(s32[16]{0:T(128)S(1)} %bitcast_dynamic-update-slice_fusion), channel_id=2, replica_groups=mesh['tower'=2,'seq'=8,'rep'=8] {'tower','seq'}, use_global_device_ids=true, to_apply=%add | all-reduce | flops 16 | bytes 128
  31.3 45.3 %all-gather.4.cloned.1.call-done = bf16[6144,3,128]{0,2,1:T(8,128)(2,1)} async-done(((bf16[384,3,128]{0,2,1:T(8,128)(2,1)}), bf16[6144,3,128]{0,2,1:T(8,128)(2,1)}) %all-gather.4.cloned.1.call-update) | async-done | bytes 4718608 | tf_op jit(solution)/shard_map/all_gather | solution.py:84
  76.7 8.2 %reshape.154 = bf16[2,3072,3,128]{1,0,3,2:T(2,128)(2,1)} reshape(bf16[6144,3,128]{0,2,1:T(8,128)(2,1)} %all-gather.4.cloned.1.call-done) | data formatting | bytes 9437184 | tf_op jit(solution)/shard_map/reshape | solution.py:87
  84.8 54.3 %all-gather.6.cloned.1.call-done = bf16[6144,3,128]{0,2,1:T(8,128)(2,1)} async-done(((bf16[384,3,128]{0,2,1:T(8,128)(2,1)}), bf16[6144,3,128]{0,2,1:T(8,128)(2,1)}) %all-gather.6.cloned.1.call-update) | async-done | bytes 4718608 | tf_op jit(solution)/shard_map/all_gather | solution.py:85
  139.1 8.2 %reshape.155 = bf16[2,3072,3,128]{1,0,3,2:T(2,128)(2,1)} reshape(bf16[6144,3,128]{0,2,1:T(8,128)(2,1)} %all-gather.6.cloned.1.call-done) | data formatting | bytes 9437184 | tf_op jit(solution)/shard_map/reshape | solution.py:88
  148.1 535.1 %while.20 = (s32[]{:T(128)}, bf16[384,3,128]{0,2,1:T(8,128)(2,1)}, bf16[384,3,128]{0,2,1:T(8,128)(2,1)}, bf16[384,3,128]{0,2,1:T(8,128)(2,1)}, bf16[384,3,128]{0...) while((s32[]{:T(128)}, bf16[384,3,128]{0,2,1:T(8,128)(2,1)}, ...), condition=%wide.region_9.10_spmd.clone, body=%wide.region_0.9_spmd.sunk.clone | while | flops 3654302208 | bytes 183187984 | solution.py:125
  148.1 5.5 constant_dynamic-slice_fusion.8
  153.6 3.7 copy.67
  172.1 6.1 constant_dynamic-slice_fusion.9
  178.2 4.2 copy.66
  182.5 4.2 copy.68
  188.8 2.6 fusion.137
  200.9 2.6 fusion.139
  205.1 40.9 %reduce-scatter.5.cloned.1.call-done = f32[384,128]{1,0:T(8,128)} async-done(((f32[6144,128]{1,0:T(8,128)}), f32[384,128]{1,0:T(8,128)}) %reduce-scatter.5.cloned.1.call-update) | async-done | bytes 196624 | tf_op jit(solution)/shard_map/while/body/eval_jaxpr/reduce_scatter | solution.py:107
  247.0 76.9 %reduce-scatter.3.cloned.1.call-done = f32[384,128]{1,0:T(8,128)} async-done(((f32[6144,128]{1,0:T(8,128)}), f32[384,128]{1,0:T(8,128)}) %reduce-scatter.3.cloned.1.call-update) | async-done | bytes 196624 | tf_op jit(solution)/shard_map/while/body/eval_jaxpr/reduce_scatter | solution.py:106
  326.3 5.5 constant_dynamic-slice_fusion.8
  331.8 3.7 copy.67
  350.3 6.1 constant_dynamic-slice_fusion.9
  356.4 4.3 copy.66
  360.6 4.3 copy.68
  367.1 2.6 fusion.137
  379.1 2.6 fusion.139
  383.3 41.1 %reduce-scatter.5.cloned.1.call-done = f32[384,128]{1,0:T(8,128)} async-done(((f32[6144,128]{1,0:T(8,128)}), f32[384,128]{1,0:T(8,128)}) %reduce-scatter.5.cloned.1.call-update) | async-done | bytes 196624 | tf_op jit(solution)/shard_map/while/body/eval_jaxpr/reduce_scatter | solution.py:107
  425.5 76.9 %reduce-scatter.3.cloned.1.call-done = f32[384,128]{1,0:T(8,128)} async-done(((f32[6144,128]{1,0:T(8,128)}), f32[384,128]{1,0:T(8,128)}) %reduce-scatter.3.cloned.1.call-update) | async-done | bytes 196624 | tf_op jit(solution)/shard_map/while/body/eval_jaxpr/reduce_scatter | solution.py:106
  504.7 5.5 constant_dynamic-slice_fusion.8
  510.2 3.7 copy.67
  528.7 6.1 constant_dynamic-slice_fusion.9
  534.8 4.3 copy.66
  539.0 4.3 copy.68
  545.5 2.6 fusion.137
  561.7 41.1 %reduce-scatter.5.cloned.1.call-done = f32[384,128]{1,0:T(8,128)} async-done(((f32[6144,128]{1,0:T(8,128)}), f32[384,128]{1,0:T(8,128)}) %reduce-scatter.5.cloned.1.call-update) | async-done | bytes 196624 | tf_op jit(solution)/shard_map/while/body/eval_jaxpr/reduce_scatter | solution.py:107
  603.9 76.9 %reduce-scatter.3.cloned.1.call-done = f32[384,128]{1,0:T(8,128)} async-done(((f32[6144,128]{1,0:T(8,128)}), f32[384,128]{1,0:T(8,128)}) %reduce-scatter.3.cloned.1.call-update) | async-done | bytes 196624 | tf_op jit(solution)/shard_map/while/body/eval_jaxpr/reduce_scatter | solution.py:106
  (214 shorter events, 112.2 us)
Async XLA Ops:
  7.2 5.2 copy-start.13
  7.2 69.5 %all-gather.4.cloned.1.call-start = ((), (), s32[]{:S(2)}) async-start(), calls=%async_computation.2 | async-start | bytes 5013504 | tf_op jit(solution)/shard_map/all_gather | solution.py:84
  9.1 4.9 copy-start.14
  9.2 5.0 copy-start.18
  12.3 126.8 %all-gather.6.cloned.1.call-start = ((), (), s32[]{:S(2)}) async-start(), calls=%async_computation.3 | async-start | bytes 5013504 | tf_op jit(solution)/shard_map/all_gather | solution.py:85
  30.5 54.3 %copy-start.16 = (pred[384]{0:T(512)(128)(4,1)}, pred[384]{0:T(512)(128)(4,1)S(1)}, u32[]{:S(2)}) copy-start(pred[384]{0:T(512)(128)(4,1)S(1)} %iota_compare_fusion) | copy-start | bytes 1156
  148.1 537.2 %copy-start.11 = (f32[384,64]{0,1:T(8,128)S(1)}, f32[384,64]{0,1:T(8,128)}, u32[]{:S(2)}) copy-start(f32[384,64]{0,1:T(8,128)} %copy-done.10) | copy-start | bytes 294916
  148.1 97.8 %reduce-scatter.5.cloned.1.call-start = ((), (), s32[]{:S(2)}) async-start(), calls=%async_computation.5 | async-start | bytes 3342336 | tf_op jit(solution)/shard_map/while/body/eval_jaxpr/reduce_scatter | solution.py:107
  164.0 2.8 copy-start.5
  172.1 151.9 %reduce-scatter.3.cloned.1.call-start = ((), (), s32[]{:S(2)}) async-start(), calls=%async_computation.4 | async-start | bytes 3342336 | tf_op jit(solution)/shard_map/while/body/eval_jaxpr/reduce_scatter | solution.py:106
  186.7 2.1 copy-start.1
  186.7 4.8 copy-start.7
  200.9 2.6 copy-start.3
  200.9 2.6 copy-start.6
  326.3 98.1 %reduce-scatter.5.cloned.1.call-start = ((), (), s32[]{:S(2)}) async-start(), calls=%async_computation.5 | async-start | bytes 3342336 | tf_op jit(solution)/shard_map/while/body/eval_jaxpr/reduce_scatter | solution.py:107
  342.2 2.8 copy-start.5
  350.2 152.1 %reduce-scatter.3.cloned.1.call-start = ((), (), s32[]{:S(2)}) async-start(), calls=%async_computation.4 | async-start | bytes 3342336 | tf_op jit(solution)/shard_map/while/body/eval_jaxpr/reduce_scatter | solution.py:106
  364.9 2.1 copy-start.1
  364.9 4.8 copy-start.7
  370.9 1.9 copy-start.2
  379.1 2.6 copy-start.3
  379.1 2.6 copy-start.6
  504.7 98.1 %reduce-scatter.5.cloned.1.call-start = ((), (), s32[]{:S(2)}) async-start(), calls=%async_computation.5 | async-start | bytes 3342336 | tf_op jit(solution)/shard_map/while/body/eval_jaxpr/reduce_scatter | solution.py:107
  520.6 2.8 copy-start.5
  528.6 152.2 %reduce-scatter.3.cloned.1.call-start = ((), (), s32[]{:S(2)}) async-start(), calls=%async_computation.4 | async-start | bytes 3342336 | tf_op jit(solution)/shard_map/while/body/eval_jaxpr/reduce_scatter | solution.py:106
  543.3 2.1 copy-start.1
  543.3 4.8 copy-start.7
  557.5 2.6 copy-start.3
  557.5 2.6 copy-start.6
  683.2 5.1 copy-start.9
  683.2 5.1 copy-start.17
  684.3 4.9 copy-start.15
  (13 other events, 20.2 us)
Sparse Core Ops, SparseCore 0:
  12.5 64.1 all-gather.3
  78.9 60.1 all-gather.5
  172.2 73.7 reduce-scatter.4
  249.8 74.0 reduce-scatter.2
  350.4 73.9 reduce-scatter.4
  428.3 74.0 reduce-scatter.2
  528.7 74.0 reduce-scatter.4
  606.8 73.9 reduce-scatter.2
where the time goes:
time: 699 us; the launch traced here: 697 us
  waiting for transfers between devices  454 us (65%)
  local copies, waits for them, and re-layouts  116 us (17%)
  matrix products  58.9 us (8%)
  other arithmetic  37.8 us (5%)
  between operations  14.9 us (2%)
  blocking collectives  14.8 us (2%)
    reduce_scatter x3, waiting for transfers between devices, per_head(): lax.psum_scatter(key_stack, ('tower', 'seq'), scatter_dimension=0, tiled=...  231 us
    reduce_scatter x3, waiting for transfers between devices, per_head(): lax.psum_scatter(value_stack, ('tower', 'seq'), scatter_dimension=0, tile...  123 us
    all_gather x1, waiting for transfers between devices, body(): lax.all_gather(value_heads, ('tower', 'seq'), axis=0, tiled=True)  54.3 us
    while x66, local copies, waits for them, and re-layouts  47.7 us
    all_gather x1, waiting for transfers between devices, body(): lax.all_gather(rot_keys, ('tower', 'seq'), axis=0, tiled=True)  45.3 us
    slice x3, local copies, waits for them, and re-layouts, per_head(): value_rows[1]  18.3 us
    slice x3, local copies, waits for them, and re-layouts, per_head(): key_rows[1]  16.4 us
    unnamed x1, blocking collectives  14.8 us
  transfers between devices with their start and end apart: 8, of which 8 were waited for; matrix products, arithmetic and copies ran while one was open for 16% of the time, Pallas kernels for 0%

commit v1 on v0

v1 whole, which is shorter than its diff:
```python
import math

import jax
import jax.numpy as jnp
import numpy as np
from jax import lax
from jax.experimental import pallas as pl
from jax.experimental.pallas import tpu as pltpu
from jax.sharding import PartitionSpec as P

HEAD_DIM = 128
HEADS_DEV = 3
TOK = 384
ROWS = 4 * TOK
HALF = 2 * TOK
SCALE = 1.0 / math.sqrt(HEAD_DIM)
SCALE_LOG2 = SCALE * math.log2(math.e)
MESH = pl.DeviceIdType.MESH
NN = (((1,), (0,)), ((), ()))
NT = (((1,), (1,)), ((), ()))
f32 = jnp.float32
bf16 = jnp.bfloat16

(
    K_R, K_L, V_R, V_L, K_FWD, V_FWD,
    Q_S, Q_T, Q_FWD, G_S, G_T, G_FWD,
    STATS, O_S1, O_S3, O_T, DQ_S1, DQ_S3, DQ_T,
    DK3, DV3, DV2, DK1, DK2, DV1,
    LEN_R, LEN_L, LEN_FWD,
) = range(28)


def dot(a, b, dims):
    return lax.dot_general(a, b, dims, preferred_element_type=f32)


def kernel(
    q_in, k_in, v_in, g_in, pos_in, len_in, rate_in,
    o_out, dq_out, dk_out, dv_out,
    kbuf, vbuf, ktbuf, vtbuf, qt, gt, lens,
    score, prob, dscore, gts,
    stat_out, stat_in, oq_own, oq_send, oq_recv,
    kv_own, kv_send, kv_recv, tables,
    send_sem, recv_sem,
):
    t, s, r = lax.axis_index("tower"), lax.axis_index("seq"), lax.axis_index("rep")
    right = (t, lax.rem(s + 2, 8), r)
    left = (t, lax.rem(s + 6, 8), r)
    sibling = (t, s + 1 - 2 * lax.rem(s, 2), r)
    peer = (1 - t, s, r)

    def copy(kind, h, src, dst, target):
        return pltpu.make_async_remote_copy(
            src_ref=src, dst_ref=dst,
            send_sem=send_sem.at[kind, h], recv_sem=recv_sem.at[kind, h],
            device_id=target, device_id_type=MESH,
        )

    def rows(slot):
        return pl.ds(slot * TOK, TOK)

    def describe(kind, h):
        own, first, second, third = rows(0), rows(1), rows(2), rows(3)
        cols = pl.ds(h * HEAD_DIM, HEAD_DIM)
        table = {
            K_R: lambda: (kbuf.at[h, own], kbuf.at[h, first], right),
            K_L: lambda: (kbuf.at[h, own], kbuf.at[h, second], left),
            V_R: lambda: (vbuf.at[h, own], vbuf.at[h, first], right),
            V_L: lambda: (vbuf.at[h, own], vbuf.at[h, second], left),
            K_FWD: lambda: (kbuf.at[h, first], kbuf.at[h, third], right),
            V_FWD: lambda: (vbuf.at[h, second], vbuf.at[h, third], left),
            Q_S: lambda: (qt.at[h, :, own], qt.at[h, :, first], sibling),
            Q_T: lambda: (qt.at[h, :, own], qt.at[h, :, second], peer),
            Q_FWD: lambda: (qt.at[h, :, second], qt.at[h, :, third], sibling),
            G_S: lambda: (gt.at[h, :, own], gt.at[h, :, first], sibling),
            G_T: lambda: (gt.at[h, :, own], gt.at[h, :, second], peer),
            G_FWD: lambda: (gt.at[h, :, second], gt.at[h, :, third], sibling),
            STATS: lambda: (stat_out.at[h], stat_in.at[h], sibling),
            O_S1: lambda: (oq_send.at[h, 0, 0], oq_recv.at[h, 0, 0], sibling),
            O_S3: lambda: (oq_send.at[h, 0, 1], oq_recv.at[h, 0, 1], sibling),
            O_T: lambda: (oq_send.at[h, 0, 2], oq_recv.at[h, 0, 2], peer),
            DQ_S1: lambda: (oq_send.at[h, 1, 0], oq_recv.at[h, 1, 0], sibling),
            DQ_S3: lambda: (oq_send.at[h, 1, 1], oq_recv.at[h, 1, 1], sibling),
            DQ_T: lambda: (oq_send.at[h, 1, 2], oq_recv.at[h, 1, 2], peer),
            DK3: lambda: (kv_send.at[h, 0], kv_recv.at[h, 0], right),
            DV3: lambda: (kv_send.at[h, 1], kv_recv.at[h, 1], left),
            DV2: lambda: (kv_send.at[h, 2], kv_recv.at[h, 2], right),
            DK1: lambda: (kv_send.at[h, 3], kv_recv.at[h, 3], left),
            DK2: lambda: (kv_send.at[h, 4], kv_recv.at[h, 4], right),
            DV1: lambda: (kv_send.at[h, 5], kv_recv.at[h, 5], left),
            LEN_R: lambda: (lens.at[0], lens.at[1], right),
            LEN_L: lambda: (lens.at[0], lens.at[2], left),
            LEN_FWD: lambda: (lens.at[1], lens.at[3], right),
        }
        return copy(kind, h, *table[kind]())

    def start(kind, h):
        describe(kind, h).start()

    def arrived(kind, h):
        describe(kind, h).wait_recv()

    barrier = pltpu.get_barrier_semaphore()
    for device in (right, left, sibling, peer):
        pl.semaphore_signal(barrier, inc=1, device_id=device, device_id_type=MESH)

    length = len_in[...]
    lens[0] = jnp.broadcast_to(length, (8, 128))
    for h in range(HEADS_DEV):
        vbuf[h, 0:TOK, :] = v_in[0, :, h * HEAD_DIM : (h + 1) * HEAD_DIM]

    pl.semaphore_wait(barrier, 4)
    start(V_R, 0)
    start(V_L, 0)
    start(LEN_R, 0)
    start(LEN_L, 0)

    angles = rate_in[:, 0:1] * pos_in[...].astype(f32)
    cos, sin = jnp.cos(angles), jnp.sin(angles)
    tables[0:64, :] = cos
    tables[64:128, :] = sin
    turned = jnp.transpose(tables[...])
    swapped = pltpu.roll(turned, 64, 1)
    low = lax.broadcasted_iota(jnp.int32, (TOK, HEAD_DIM), 1) < 64
    cos_rows = jnp.where(low, turned, swapped)
    sin_rows = jnp.where(low, -swapped, turned)
    present_rows = lax.broadcasted_iota(jnp.int32, (TOK, HEAD_DIM), 0) < length
    present_cols = lax.broadcasted_iota(jnp.int32, (1, TOK), 1) < length

    def prepare_keys(h):
        key = k_in[0, :, h * HEAD_DIM : (h + 1) * HEAD_DIM].astype(f32)
        key = key * cos_rows + pltpu.roll(key, 64, 1) * sin_rows
        key = jnp.where(present_rows, key, key[0:1, :])
        kbuf[h, 0:TOK, :] = key.astype(bf16)

    def prepare_queries(h):
        cols = slice(h * HEAD_DIM, (h + 1) * HEAD_DIM)
        query = jnp.transpose(q_in[0, :, cols].astype(f32))
        x1, x2 = query[0:64, :], query[64:128, :]
        qt[h, 0:64, 0:TOK] = (x1 * cos - x2 * sin).astype(bf16)
        qt[h, 64:128, 0:TOK] = (x2 * cos + x1 * sin).astype(bf16)
        grad = jnp.transpose(g_in[0, :, cols].astype(f32))
        gt[h, :, 0:TOK] = jnp.where(present_cols, grad, 0.0).astype(bf16)

    def send_keys(h):
        start(K_R, h)
        start(K_L, h)

    def send_values(h):
        start(V_R, h)
        start(V_L, h)

    def send_queries(h):
        start(Q_T, h)
        start(Q_S, h)
        start(G_T, h)
        start(G_S, h)

    def forward_keys(h):
        arrived(K_R, h)
        start(K_FWD, h)
        arrived(V_L, h)
        start(V_FWD, h)

    def forward_queries(h):
        arrived(Q_T, h)
        start(Q_FWD, h)
        arrived(G_T, h)
        start(G_FWD, h)

    prepare_keys(0)
    send_keys(0)
    prepare_queries(0)
    send_queries(0)
    for h in (1, 2):
        prepare_keys(h)
        prepare_queries(h)
    arrived(LEN_R, 0)
    start(LEN_FWD, 0)
    forward_keys(0)
    forward_queries(0)
    for h in (1, 2):
        send_values(h)
        send_keys(h)
        send_queries(h)
    arrived(LEN_L, 0)
    arrived(LEN_FWD, 0)

    def valid_row(slot):
        return (
            lax.broadcasted_iota(jnp.int32, (1, TOK), 1) < lens[slot][0:1, 0:1]
        ).astype(f32)

    def turn_keys(h, slot):
        valid = valid_row(slot)
        cols = rows(slot)
        ktbuf[:, cols] = (jnp.transpose(kbuf[h, cols, :].astype(f32)) * valid).astype(bf16)
        vtbuf[0:128, cols] = (jnp.transpose(vbuf[h, cols, :].astype(f32)) * valid).astype(bf16)
        vtbuf[128:144, cols] = jnp.broadcast_to(valid, (16, TOK)).astype(bf16)

    def forward_half(h, half):
        cols = pl.ds(half * HALF, HALF)
        query = qt[h, :, cols]
        top = None
        for slot in range(4):
            if half == 0:
                if slot == 1:
                    arrived(V_R, h)
                if slot == 2:
                    arrived(K_L, h)
                if slot == 3:
                    arrived(K_FWD, h)
            part = dot(kbuf[h, rows(slot), :], query, NN)
            score[rows(slot), :] = part
            part = jnp.max(part.reshape(TOK // 8, 8, HALF), axis=0)
            top = part if top is None else jnp.maximum(top, part)
        top = jnp.max(top, axis=0, keepdims=True) * SCALE_LOG2
        if half == 0:
            arrived(V_FWD, h)
            for slot in range(4):
                turn_keys(h, slot)
        for slot in range(4):
            prob[rows(slot), cols] = jnp.exp2(score[rows(slot), :] * SCALE_LOG2 - top).astype(bf16)
        out = dot(vtbuf[...], prob[:, cols], NN)
        oq_own[h, 0, :, cols] = out[0:128, :]
        inner = jnp.sum(out[0:128, :] * gt[h, :, cols].astype(f32), axis=0, keepdims=True)
        stat_out[h, 0:1, cols] = top
        stat_out[h, 1:2, cols] = out[128:129, :]
        stat_out[h, 2:3, cols] = inner

    def normalise(h):
        mine = stat_out[h]
        other = stat_in[h]
        other = jnp.concatenate(
            [other[:, TOK : 2 * TOK], other[:, 0:TOK], other[:, 3 * TOK :], other[:, 2 * TOK : 3 * TOK]],
            axis=1,
        )
        top = jnp.maximum(mine[0:1], other[0:1])
        grow_mine, grow_other = jnp.exp2(mine[0:1] - top), jnp.exp2(other[0:1] - top)
        inverse = 1.0 / (mine[1:2] * grow_mine + other[1:2] * grow_other)
        factor, factor_other = grow_mine * inverse, grow_other * inverse
        row_dot = (factor * mine[2:3] + factor_other * other[2:3]) * factor
        return factor, row_dot

    def share(h, which):
        oq_send[h, which, 0] = oq_own[h, which, :, TOK : 2 * TOK].astype(bf16)
        start((O_S1, DQ_S1)[which], h)
        oq_send[h, which, 1] = oq_own[h, which, :, 3 * TOK :].astype(bf16)
        start((O_S3, DQ_S3)[which], h)

    def pass_on(h, which):
        arrived((O_S3, DQ_S3)[which], h)
        both = oq_own[h, which, :, 2 * TOK : 3 * TOK] + oq_recv[h, which, 1].astype(f32)
        oq_send[h, which, 2] = both.astype(bf16)
        start((O_T, DQ_T)[which], h)

    def finish_queries(h, which):
        arrived((O_S1, DQ_S1)[which], h)
        arrived((O_T, DQ_T)[which], h)
        total = oq_own[h, which, :, 0:TOK] + oq_recv[h, which, 0].astype(f32)
        total = (total + oq_recv[h, which, 2].astype(f32)).astype(bf16).astype(f32)
        cols = slice(h * HEAD_DIM, (h + 1) * HEAD_DIM)
        if which == 0:
            o_out[0, :, cols] = jnp.transpose(jnp.where(present_cols, total, 0.0)).astype(bf16)
        else:
            dq_out[0, :, cols] = jnp.transpose(unrotate(total)).astype(bf16)

    def unrotate(total):
        cos, sin = tables[0:64, :], tables[64:128, :]
        d1, d2 = total[0:64, :], total[64:128, :]
        return jnp.concatenate([d1 * cos + d2 * sin, d2 * cos - d1 * sin], axis=0)

    def backward(h):
        factor, row_dot = normalise(h)
        gts[...] = (gt[h].astype(f32) * factor).astype(bf16)
        oq_own[h, 0] = oq_own[h, 0] * factor
        share(h, 0)
        for pair in (1, 0):
            keys = pl.ds(pair * HALF, HALF)
            value = vbuf[h, keys, :]
            for half in range(2):
                cols = pl.ds(half * HALF, HALF)
                grad = dot(value, gts[:, cols], NN)
                grad = prob[keys, cols].astype(f32) * (grad - row_dot[:, half * HALF : (half + 1) * HALF])
                dscore[keys, cols] = grad.astype(bf16)
            dv = dot(gts[...], prob[keys, :], NT)
            dk = dot(qt[h], dscore[keys, :], NT) * SCALE
            if pair == 1:
                kv_send[h, 0] = dk[:, TOK:].astype(bf16)
                start(DK3, h)
                kv_send[h, 1] = dv[:, TOK:].astype(bf16)
                start(DV3, h)
                kv_send[h, 2] = dv[:, 0:TOK].astype(bf16)
                start(DV2, h)
                kv_own[h, 2] = dk[:, 0:TOK]
            else:
                kv_send[h, 3] = dk[:, TOK:].astype(bf16)
                start(DK1, h)
                kv_own[h, 3] = dv[:, TOK:]
                kv_own[h, 0] = dk[:, 0:TOK]
                kv_own[h, 1] = dv[:, 0:TOK]
        oq_own[h, 1] = dot(ktbuf[...], dscore[...], NN) * SCALE
        share(h, 1)

    def reduce_keys(h):
        arrived(DK3, h)
        kv_send[h, 4] = (kv_own[h, 2] + kv_recv[h, 0].astype(f32)).astype(bf16)
        start(DK2, h)
        arrived(DV3, h)
        kv_send[h, 5] = (kv_own[h, 3] + kv_recv[h, 1].astype(f32)).astype(bf16)
        start(DV1, h)

    def finish_keys(h):
        cols = slice(h * HEAD_DIM, (h + 1) * HEAD_DIM)
        arrived(DK1, h)
        arrived(DK2, h)
        total = kv_own[h, 0] + kv_recv[h, 3].astype(f32) + kv_recv[h, 4].astype(f32)
        total = jnp.where(present_cols, total, 0.0).astype(bf16).astype(f32)
        dk_out[0, :, cols] = jnp.transpose(unrotate(total)).astype(bf16)
        arrived(DV2, h)
        arrived(DV1, h)
        total = kv_own[h, 1] + kv_recv[h, 2].astype(f32) + kv_recv[h, 5].astype(f32)
        dv_out[0, :, cols] = jnp.transpose(jnp.where(present_cols, total, 0.0)).astype(bf16)

    for h in range(HEADS_DEV):
        arrived(Q_S, h)
        arrived(G_S, h)
        forward_half(h, 0)
        if h > 0:
            pass_on(h - 1, 0)
            pass_on(h - 1, 1)
            reduce_keys(h - 1)
        if h + 1 < HEADS_DEV:
            forward_keys(h + 1)
            forward_queries(h + 1)
        arrived(Q_FWD, h)
        arrived(G_FWD, h)
        forward_half(h, 1)
        start(STATS, h)
        if h > 0:
            finish_queries(h - 1, 0)
            finish_queries(h - 1, 1)
            finish_keys(h - 1)
        arrived(STATS, h)
        backward(h)
    last = HEADS_DEV - 1
    pass_on(last, 0)
    reduce_keys(last)
    pass_on(last, 1)
    finish_queries(last, 0)
    finish_queries(last, 1)
    finish_keys(last)
    for h in range(HEADS_DEV):
        for kind in range(LEN_R):
            describe(kind, h).wait_send()
    for kind in (LEN_R, LEN_L, LEN_FWD):
        describe(kind, 0).wait_send()


def body(queries, key_input, values, cotangent, positions, lengths):
    rates = np.exp(-math.log(10000.0) * np.arange(64, dtype=np.float64) / 64).astype(np.float32)
    rates = jnp.asarray(np.broadcast_to(rates[:, None], (64, 128)))
    shape = jax.ShapeDtypeStruct(queries.shape, bf16)
    vmem = pl.BlockSpec(memory_space=pltpu.VMEM)
    block = (HEAD_DIM, TOK)
    n = HEADS_DEV
    return pl.pallas_call(
        kernel,
        out_shape=[shape] * 4,
        in_specs=[vmem] * 7,
        out_specs=[vmem] * 4,
        scratch_shapes=[
            pltpu.VMEM((n, ROWS, HEAD_DIM), bf16),
            pltpu.VMEM((n, ROWS, HEAD_DIM), bf16),
            pltpu.VMEM((HEAD_DIM, ROWS), bf16),
            pltpu.VMEM((HEAD_DIM + 16, ROWS), bf16),
            pltpu.VMEM((n, HEAD_DIM, ROWS), bf16),
            pltpu.VMEM((n, HEAD_DIM, ROWS), bf16),
            pltpu.VMEM((4, 8, 128), jnp.int32),
            pltpu.VMEM((ROWS, HALF), f32),
            pltpu.VMEM((ROWS, ROWS), bf16),
            pltpu.VMEM((ROWS, ROWS), bf16),
            pltpu.VMEM((HEAD_DIM, ROWS), bf16),
            pltpu.VMEM((n, 8, ROWS), f32),
            pltpu.VMEM((n, 8, ROWS), f32),
            pltpu.VMEM((n, 2, HEAD_DIM, ROWS), f32),
            pltpu.VMEM((n, 2, 3) + block, bf16),
            pltpu.VMEM((n, 2, 3) + block, bf16),
            pltpu.VMEM((n, 4) + block, f32),
            pltpu.VMEM((n, 6) + block, bf16),
            pltpu.VMEM((n, 6) + block, bf16),
            pltpu.VMEM(block, f32),
            pltpu.SemaphoreType.DMA((28, n)),
            pltpu.SemaphoreType.DMA((28, n)),
        ],
        compiler_params=pltpu.CompilerParams(
            collective_id=0, has_side_effects=True, vmem_limit_bytes=60 * 1024 * 1024
        ),
        cost_estimate=pl.CostEstimate(
            flops=12 * n * ROWS * ROWS * HEAD_DIM, bytes_accessed=16 << 20, transcendentals=n * ROWS * ROWS
        ),
        name="attention",
    )(queries, key_input, values, cotangent, positions, lengths, rates)


def solution(mesh):
    split = P("tower", "seq", "rep")
    return jax.shard_map(
        body,
        mesh=mesh,
        in_specs=(split, split, split, split, P("tower", "seq"), P("tower", "seq")),
        out_specs=(split, split, split, split),
        check_vma=False,
    )
```

time: 699 us -> 76.7 us (0.11)
  waiting for transfers between devices: 454 us -> 0 us
  local copies, waits for them, and re-layouts: 116 us -> 5.3 us
  Pallas kernels: 0 us -> 69.4 us
  matrix products: 58.9 us -> 0 us
  other arithmetic: 37.8 us -> 0 us
  blocking collectives: 14.8 us -> 0 us
  between operations: 14.9 us -> 1.33 us
    reduce_scatter x6 -> x0, waiting for transfers between devices: 354 us -> none  [the longest x3 231 us: per_head(): lax.psum_scatter(key_stack, ('tower', 'seq'), scatter_dimension=0, tiled=...]
    all_gather x2 -> x0, waiting for transfers between devices: 99.6 us -> none  [the longest x1 54.3 us: body(): lax.all_gather(value_heads, ('tower', 'seq'), axis=0, tiled=True)]
    pallas_call x0 -> x1, Pallas kernels: none -> 69.4 us  [body(): pl.pallas_call(kernel, out_shape=[shape] * 4, in_specs=[vmem] * 7, out_sp...]
    dot_general x36 -> x0, matrix products: 58.9 us -> none  [the longest x6 14.2 us: branch(): jnp.dot(probabilities, value_rows, preferred_element_type=jnp.float32)]
    while x66 -> x0, local copies, waits for them, and re-layouts: 47.7 us -> none
    slice x9 -> x0, local copies, waits for them, and re-layouts: 35 us -> none  [the longest x3 18.3 us: per_head(): value_rows[1]]
    reshape x2 -> x0, local copies, waits for them, and re-layouts: 16.4 us -> none  [the longest x1 8.24 us: body(): val_heads = joined_values.reshape(2, -1, head_count, HEAD_DIM)]
    unnamed x1 -> x0, blocking collectives: 14.8 us -> none
  transfers between devices with their start and end apart: 8 -> 0, of which waited for: 8 -> 0; matrix products, arithmetic and copies ran while one was open for 16% -> 0% of each run, Pallas kernels for 0% -> 0%
where the time goes in v1:
time: 76.7 us; the launch traced here: 76.1 us
  Pallas kernels  69.4 us (90%)
  local copies, waits for them, and re-layouts  5.3 us (7%)
  between operations  1.33 us (2%)
    pallas_call x1, Pallas kernels, body(): pl.pallas_call(kernel, out_shape=[shape] * 4, in_specs=[vmem] * 7, out_sp...  69.4 us
    unnamed x12, local copies, waits for them, and re-layouts  4.61 us

profile of v1, /device:TPU:0, one launch (start us, length us, event | category | flops | bytes accessed | tf_op | source)
XLA Modules:
  0.0 76.1 jit_solution(15776720180707592879)
XLA Ops:
  0.6 0.0 copy-start.3
  1.3 0.0 copy-done.3
  1.3 0.7 jit_solution_.3.rate_in
  2.0 69.4 %attention.1 = (bf16[1,384,384]{2,1,0:T(8,128)(2,1)}, bf16[1,384,384]{2,1,0:T(8,128)(2,1)}, bf16[1,384,384]{2,1,0:T(8,128)(2,1)}, bf16[1,384,384]{2,1,0:T(8,128)(2,1)}) custom-call(bf16[1,384,384]{2,1,0:T(8,128)(2,1)} %q_in.1, bf16[1,384,384]{2,1,0:T(8,128)(2,1)} %k_in.1, bf16[1,384,384]{2,1,0:T(8,128)(2,1)} %v_in.1, bf16[1,384,384]{2,1,0:T(8,128)(2,1)} %g_in.1, ...), custom_call_target="tpu_custom_call" | custom-call | flops 10871635968 | bytes 16777216 | tf_op jit(solution)/shard_map/attention/pallas_call | solution.py:367
  71.5 0.0 copy-start.2
  71.5 1.7 %copy.16 = bf16[1,384,384]{2,1,0:T(8,128)(2,1)} copy(bf16[1,384,384]{2,1,0:T(8,128)(2,1)} %get-tuple-element.8) | data formatting | bytes 589824
  73.2 0.0 copy-done.2
  73.2 0.0 copy-start.1
  73.2 0.7 copy.17
  73.9 0.4 copy-done.1
  74.3 0.0 copy-start
  74.3 0.7 copy.18
  75.0 0.4 copy-done
  75.4 0.7 copy.19
Async XLA Ops:
  0.6 0.7 copy-start.3
  71.5 1.8 %copy-start.2 = (bf16[1,384,384]{2,1,0:T(8,128)(2,1)S(1)}, bf16[1,384,384]{2,1,0:T(8,128)(2,1)}, u32[]{:S(2)}) copy-start(bf16[1,384,384]{2,1,0:T(8,128)(2,1)} %get-tuple-element.9) | copy-start | bytes 884740
  73.2 1.1 %copy-start.1 = (bf16[1,384,384]{2,1,0:T(8,128)(2,1)S(1)}, bf16[1,384,384]{2,1,0:T(8,128)(2,1)}, u32[]{:S(2)}) copy-start(bf16[1,384,384]{2,1,0:T(8,128)(2,1)} %get-tuple-element.10) | copy-start | bytes 884740
  74.3 1.1 %copy-start = (bf16[1,384,384]{2,1,0:T(8,128)(2,1)S(1)}, bf16[1,384,384]{2,1,0:T(8,128)(2,1)}, u32[]{:S(2)}) copy-start(bf16[1,384,384]{2,1,0:T(8,128)(2,1)} %get-tuple-element.11) | copy-start | bytes 884740

commit v2 on v0

v2 whole, which is shorter than its diff:
```python
import math

import jax
import jax.numpy as jnp
from jax import lax
from jax.experimental import pallas as pl
from jax.experimental.pallas import tpu as pltpu
from jax.sharding import PartitionSpec as P

HEAD_DIM = 128
HEADS_DEV = 3
TOK = 384
ROWS = 4 * TOK
HALF = 2 * TOK
QCOLS = 12 * TOK
N_SEM = 80
SCALE = 1.0 / math.sqrt(HEAD_DIM)
SCALE_LOG2 = SCALE * math.log2(math.e)
MESH = pl.DeviceIdType.MESH
NN = (((1,), (0,)), ((), ()))
f32 = jnp.float32
bf16 = jnp.bfloat16


def dot(a, b):
    return lax.dot_general(a, b, NN, preferred_element_type=f32)


def rows(slot):
    return pl.ds(slot * TOK, TOK)


def kernel(
    q_hbm, k_hbm, v_hbm, g_hbm, pos_in, len_in,
    o_hbm, dq_hbm, dk_hbm, dv_hbm,
    ins, outs, in_sem, out_sem,
    khead, vhead, qhead, ghead,
    kbuf, vbuf, ktbuf, vtbuf, qt, gt, qr, gr, gts, lens,
    score, prob, dscore,
    stat_out, stat_in, oq_own, oq_send, oq_recv, oq_mate_send, oq_mate_recv,
    kv_own, kv_send, kv_recv, tables,
    send_sem, recv_sem,
):
    t, s, r = lax.axis_index("tower"), lax.axis_index("seq"), lax.axis_index("rep")
    x = s // 2
    odd = lax.rem(x, 2)
    mate = (t, s + 2 - 4 * odd, r)
    cross = (t, lax.rem(s + 6 + 4 * odd, 8), r)
    sibling = (t, s + 1 - 2 * lax.rem(s, 2), r)
    peer = (1 - t, s, r)
    mine = 2 * lax.rem((x + 1) // 2, 2)
    theirs = 2 - mine

    loads = {}
    for n, (name, src) in enumerate((("k", k_hbm), ("q", q_hbm), ("v", v_hbm), ("g", g_hbm))):
        loads[name] = pltpu.make_async_copy(src.at[0], ins.at[n], in_sem.at[n])
        loads[name].start()
    k_in, q_in, v_in, g_in = (ins.at[n] for n in range(4))
    stores = []

    def store(n, out, h, block):
        outs[n, :, head_cols(h)] = block
        copy = pltpu.make_async_copy(
            outs.at[n, :, head_cols(h)], out.at[0, :, head_cols(h)], out_sem.at[len(stores)]
        )
        copy.start()
        stores.append(copy)

    copies = {}

    def plan(name, src, dst, target):
        n = len(copies)
        copies[name] = pltpu.make_async_remote_copy(
            src_ref=src, dst_ref=dst, send_sem=send_sem.at[n], recv_sem=recv_sem.at[n],
            device_id=target, device_id_type=MESH,
        )

    def start(*names):
        for name in names:
            copies[name].start()

    def arrived(*names):
        for name in names:
            copies[name].wait_recv()

    plan("k_m", khead.at[theirs], kbuf.at[0, rows(1)], mate)
    plan("v_m", vhead.at[theirs], vbuf.at[0, rows(1)], mate)
    plan("q_m", qhead.at[theirs], qt.at[:, rows(4)], mate)
    plan("g_m", ghead.at[theirs], gt.at[:, rows(4)], mate)
    plan("k_c", khead.at[mine], kbuf.at[0, rows(2)], cross)
    plan("v_c", vhead.at[mine], vbuf.at[0, rows(2)], cross)
    plan("k_f", kbuf.at[0, rows(1)], kbuf.at[0, rows(3)], cross)
    plan("v_f", vbuf.at[0, rows(1)], vbuf.at[0, rows(3)], cross)
    plan("k1_m", khead.at[1], kbuf.at[1, rows(1)], mate)
    plan("v1_m", vhead.at[1], vbuf.at[1, rows(1)], mate)
    plan("k1_c", khead.at[1], kbuf.at[1, rows(2)], cross)
    plan("v1_c", vhead.at[1], vbuf.at[1, rows(2)], cross)
    plan("k1_f", kbuf.at[1, rows(1)], kbuf.at[1, rows(3)], cross)
    plan("v1_f", vbuf.at[1, rows(2)], vbuf.at[1, rows(3)], mate)
    plan("l_m", lens.at[0], lens.at[1], mate)
    plan("l_c", lens.at[0], lens.at[2], cross)
    plan("l_f", lens.at[1], lens.at[3], cross)
    for v in range(3):
        for name, buf in (("q", qt), ("g", gt)):
            plan((name + "_s", v), buf.at[:, rows(4 * v)], buf.at[:, rows(4 * v + 1)], sibling)
            plan((name + "_t", v), buf.at[:, rows(4 * v)], buf.at[:, rows(4 * v + 2)], peer)
            plan((name + "_f", v), buf.at[:, rows(4 * v + 2)], buf.at[:, rows(4 * v + 3)], sibling)
        for w in range(2):
            plan(("o_s1", v, w), oq_send.at[v, w, 0], oq_recv.at[v, w, 0], sibling)
            plan(("o_s3", v, w), oq_send.at[v, w, 1], oq_recv.at[v, w, 1], sibling)
            plan(("o_t", v, w), oq_send.at[v, w, 2], oq_recv.at[v, w, 2], peer)
    for half in range(6):
        plan(("st", half), stat_out.at[half], stat_in.at[half], sibling)
    for w in range(2):
        plan(("o_m", w), oq_mate_send.at[w], oq_mate_recv.at[w], mate)
        plan(("p2", w), kv_send.at[0, w, 0], kv_recv.at[0, w, 0], cross)
        plan(("p3", w), kv_send.at[0, w, 1], kv_recv.at[0, w, 1], cross)
        plan(("p1", w), kv_send.at[0, w, 2], kv_recv.at[0, w, 2], mate)
        plan(("s3", w), kv_send.at[1, w, 0], kv_recv.at[1, w, 0], (cross, mate)[w])
        plan(("s1", w), kv_send.at[1, w, 1], kv_recv.at[1, w, 1], mate)
        plan(("s2", w), kv_send.at[1, w, 2], kv_recv.at[1, w, 2], cross)

    barrier = pltpu.get_barrier_semaphore()
    for device in (mate, cross, sibling, peer):
        pl.semaphore_signal(barrier, inc=1, device_id=device, device_id_type=MESH)

    length = len_in[...]
    lens[0] = jnp.broadcast_to(length, (8, 128))
    exponent = lax.broadcasted_iota(jnp.int32, (64, TOK), 0).astype(f32)
    angles = jnp.exp(-math.log(10000.0) * exponent / 64) * pos_in[...].astype(f32)
    cos, sin = jnp.cos(angles), jnp.sin(angles)
    tables[0:64, :] = cos
    tables[64:128, :] = sin
    turned = jnp.transpose(tables[...])
    swapped = pltpu.roll(turned, 64, 1)
    low = lax.broadcasted_iota(jnp.int32, (TOK, HEAD_DIM), 1) < 64
    tables_rows = jnp.where(low, turned, swapped), jnp.where(low, -swapped, turned)
    present_rows = lax.broadcasted_iota(jnp.int32, (TOK, HEAD_DIM), 0) < length
    present_cols = lax.broadcasted_iota(jnp.int32, (1, TOK), 1) < length

    def prepare_keys(h):
        cos_rows, sin_rows = tables_rows
        key = k_in[:, h * HEAD_DIM : (h + 1) * HEAD_DIM].astype(f32)
        key = key * cos_rows + pltpu.roll(key, 64, 1) * sin_rows
        key = jnp.where(present_rows, key, key[0:1, :])
        khead[h] = key.astype(bf16)

    def prepare_queries(h):
        cols = slice(h * HEAD_DIM, (h + 1) * HEAD_DIM)
        query = jnp.transpose(q_in[:, cols].astype(f32))
        x1, x2 = query[0:64, :], query[64:128, :]
        qhead[h, 0:64, :] = (x1 * cos - x2 * sin).astype(bf16)
        qhead[h, 64:128, :] = (x2 * cos + x1 * sin).astype(bf16)
        grad = jnp.transpose(g_in[:, cols].astype(f32))
        ghead[h] = jnp.where(present_cols, grad, 0.0).astype(bf16)

    loads["k"].wait()
    prepare_keys(0)
    prepare_keys(2)
    pl.semaphore_wait(barrier, 4)
    start("k_m", "k_c", "l_m", "l_c")
    kbuf[0, 0:TOK, :] = khead[mine]
    loads["q"].wait()
    loads["g"].wait()
    prepare_queries(0)
    prepare_queries(2)
    start("q_m")
    qt[:, 0:TOK] = qhead[mine]
    start(("q_s", 0), ("q_t", 0))
    loads["v"].wait()
    for h in range(HEADS_DEV):
        vhead[h] = v_in[:, h * HEAD_DIM : (h + 1) * HEAD_DIM]
    start("v_m", "g_m")
    gt[:, 0:TOK] = ghead[mine]
    start(("g_s", 0), ("g_t", 0))
    vbuf[0, 0:TOK, :] = vhead[mine]
    arrived("l_m")
    start("l_f")

    def valid_row(slot):
        return (
            lax.broadcasted_iota(jnp.int32, (1, TOK), 1) < lens[slot][0:1, 0:1]
        ).astype(f32)

    def turn_keys(st, slot):
        valid = valid_row(slot)
        cols = rows(slot)
        ktbuf[st, :, cols] = (jnp.transpose(kbuf[st, cols, :].astype(f32)) * valid).astype(bf16)

    def turn_values(st, slot):
        valid = valid_row(slot)
        cols = rows(slot)
        vtbuf[st, 0:128, cols] = (jnp.transpose(vbuf[st, cols, :].astype(f32)) * valid).astype(bf16)
        vtbuf[st, 128:144, cols] = jnp.broadcast_to(valid, (16, TOK)).astype(bf16)

    def cols_of(half):
        return pl.ds(half * HALF, HALF)

    def prob_cols(half):
        return pl.ds((half % 4) * HALF, HALF)

    def scores(st, half, before=None):
        query = qt[:, cols_of(half)]
        top = None
        for slot in range(4):
            if before is not None:
                before(slot)
            part = dot(kbuf[st, rows(slot), :], query)
            score[half % 2, rows(slot), :] = part
            part = jnp.max(part.reshape(TOK // 8, 8, HALF), axis=0)
            top = part if top is None else jnp.maximum(top, part)
        top = jnp.max(top, axis=0, keepdims=True) * SCALE_LOG2
        stat_out[half, 0:1, :] = top
        for slot in range(4):
            prob[rows(slot), prob_cols(half)] = jnp.exp2(
                score[half % 2, rows(slot), :] * SCALE_LOG2 - top
            ).astype(bf16)

    def outputs(st, half):
        cols = cols_of(half)
        out = dot(vtbuf[st], prob[:, prob_cols(half)])
        oq_own[0, :, cols] = out[0:128, :]
        stat_out[half, 1:2, :] = out[128:129, :]
        stat_out[half, 2:3, :] = jnp.sum(
            out[0:128, :] * gt[:, cols].astype(f32), axis=0, keepdims=True
        )
        start(("st", half))

    def turn_queries(half):
        qr[cols_of(half), :] = jnp.transpose(qt[:, cols_of(half)].astype(f32)).astype(bf16)

    def normalise(half):
        arrived(("st", half))
        mine_, other = stat_out[half], stat_in[half]
        other = jnp.concatenate([other[:, TOK:], other[:, 0:TOK]], axis=1)
        top = jnp.maximum(mine_[0:1], other[0:1])
        grow, grow_other = jnp.exp2(mine_[0:1] - top), jnp.exp2(other[0:1] - top)
        inverse = 1.0 / (mine_[1:2] * grow + other[1:2] * grow_other)
        factor, factor_other = grow * inverse, grow_other * inverse
        row_dot = (factor * mine_[2:3] + factor_other * other[2:3]) * factor
        cols = cols_of(half)
        scaled = gt[:, cols].astype(f32) * factor
        gts[:, cols] = scaled.astype(bf16)
        gr[cols, :] = jnp.transpose(scaled).astype(bf16)
        oq_own[0, :, cols] = oq_own[0, :, cols] * factor
        return row_dot

    def share(v, w):
        oq_send[v, w, 0] = oq_own[w, :, rows(4 * v + 1)].astype(bf16)
        oq_send[v, w, 1] = oq_own[w, :, rows(4 * v + 3)].astype(bf16)
        start(("o_s3", v, w), ("o_s1", v, w))

    def pass_on(v, w):
        arrived(("o_s3", v, w))
        both = oq_own[w, :, rows(4 * v + 2)] + oq_recv[v, w, 1].astype(f32)
        oq_send[v, w, 2] = both.astype(bf16)
        start(("o_t", v, w))

    def total_queries(v, w):
        arrived(("o_s1", v, w), ("o_t", v, w))
        total = oq_own[w, :, rows(4 * v)] + oq_recv[v, w, 0].astype(f32)
        return (total + oq_recv[v, w, 2].astype(f32)).astype(bf16)

    def head_cols(h):
        if isinstance(h, int):
            return pl.ds(h * HEAD_DIM, HEAD_DIM)
        return pl.ds(pl.multiple_of(h * HEAD_DIM, HEAD_DIM), HEAD_DIM)

    def write_queries(h, w, total):
        total = total.astype(f32)
        if w == 0:
            total = jnp.where(present_cols, total, 0.0)
            store(0, o_hbm, h, jnp.transpose(total).astype(bf16))
        else:
            cos, sin = tables[0:64, :], tables[64:128, :]
            d1, d2 = total[0:64, :], total[64:128, :]
            total = jnp.concatenate([d1 * cos + d2 * sin, d2 * cos - d1 * sin], axis=0)
            store(1, dq_hbm, h, jnp.transpose(total).astype(bf16))

    def write_keys(h, w, total):
        total = jnp.where(present_rows, total.astype(f32), 0.0)
        if w == 0:
            cos_rows, sin_rows = tables_rows
            total = total.astype(bf16).astype(f32)
            total = total * cos_rows - pltpu.roll(total, 64, 1) * sin_rows
            store(2, dk_hbm, h, total.astype(bf16))
        else:
            store(3, dv_hbm, h, total.astype(bf16))

    def score_gradients(st, keys, half, row_dot):
        grad = dot(vbuf[st, keys, :], gts[:, cols_of(half)])
        grad = prob[keys, prob_cols(half)].astype(f32) * (grad - row_dot)
        dscore[keys, prob_cols(half)] = grad.astype(bf16)

    def key_gradients(st, keys, halves):
        width = pl.ds(0, len(halves) * HALF)
        queries = pl.ds(halves[0] * HALF, len(halves) * HALF)
        dk = dot(dscore[keys, width], qr[queries, :]) * SCALE
        dv = dot(prob[keys, width], gr[queries, :])
        return dk, dv

    def query_gradients(st, half):
        oq_own[1, :, cols_of(half)] = dot(ktbuf[st], dscore[:, prob_cols(half)]) * SCALE

    def relay(got, *onward):
        arrived(got)
        start(*onward)

    def before(slot):
        if slot == 1:
            relay("k_m", "k_f", "v_c")
        if slot == 2:
            relay(("q_t", 0), ("q_f", 0))
            arrived("k_c")
        if slot == 3:
            relay("q_m", ("q_s", 1), ("q_t", 1))
            arrived("k_f")

    arrived(("q_s", 0))
    scores(0, 0, before)
    relay("v_m", "v_f")
    prepare_keys(1)
    prepare_queries(1)
    kbuf[1, 0:TOK, :] = khead[1]
    vbuf[1, 0:TOK, :] = vhead[1]
    qt[:, 8 * TOK : 9 * TOK] = qhead[1]
    gt[:, 8 * TOK : 9 * TOK] = ghead[1]
    start("k1_m", "k1_c", "v1_m", "v1_c")
    relay(("g_t", 0), ("g_f", 0))
    arrived(("q_f", 0))
    scores(0, 1)
    arrived(("q_s", 1))
    scores(0, 2)
    relay("g_m", ("g_s", 1), ("g_t", 1))
    relay(("q_t", 1), ("q_f", 1))
    arrived("v_c", "l_c", "l_f", "v_f", ("g_s", 0), ("g_f", 0))
    for slot in range(4):
        turn_values(0, slot)
    outputs(0, 0)
    outputs(0, 1)
    start(("q_s", 2), ("q_t", 2), ("g_s", 2), ("g_t", 2))
    arrived(("q_f", 1))
    scores(0, 3)
    arrived(("g_s", 1))
    outputs(0, 2)
    relay(("g_t", 1), ("g_f", 1))
    for slot in range(4):
        turn_keys(0, slot)
    for half in range(4):
        turn_queries(half)
    arrived(("g_f", 1))
    outputs(0, 3)

    row_dots = [None] * 6
    for v in range(2):
        for half in (2 * v, 2 * v + 1):
            row_dots[half] = normalise(half)
        share(v, 0)
        for half in (2 * v, 2 * v + 1):
            score_gradients(0, pl.ds(HALF, HALF), half, row_dots[half])
    relay("k1_m", "k1_f")
    relay("v1_c", "v1_f")
    relay(("q_t", 2), ("q_f", 2))
    relay(("g_t", 2), ("g_f", 2))
    totals = key_gradients(0, pl.ds(HALF, HALF), (0, 1, 2, 3))
    for w in range(2):
        kv_send[0, w, 1] = totals[w][TOK:].astype(bf16)
        start(("p3", w))
    for w in range(2):
        kv_send[0, w, 0] = totals[w][0:TOK].astype(bf16)
        start(("p2", w))
    pass_on(0, 0)
    pass_on(1, 0)
    for half in range(4):
        score_gradients(0, pl.ds(0, HALF), half, row_dots[half])
    for half in (2, 3):
        query_gradients(0, half)
    share(1, 1)
    for half in (0, 1):
        query_gradients(0, half)
    share(0, 1)
    totals = key_gradients(0, pl.ds(0, HALF), (0, 1, 2, 3))
    pass_on(1, 1)
    pass_on(0, 1)
    for w, total in enumerate(totals):
        kv_own[0, w, 0] = total[0:TOK]
        kv_own[0, w, 1] = total[TOK:]

    arrived("k1_c", "k1_f", ("q_s", 2), ("q_f", 2))
    scores(1, 4)
    for w in range(2):
        arrived(("p3", w))
        kv_send[0, w, 2] = (kv_own[0, w, 1] + kv_recv[0, w, 1].astype(f32)).astype(bf16)
        start(("p1", w))
    scores(1, 5)
    oq_mate_send[0] = total_queries(1, 0)
    start(("o_m", 0))
    arrived("v1_m", "v1_f", ("g_s", 2), ("g_f", 2))
    for slot in range(4):
        turn_values(1, slot)
    outputs(1, 4)
    outputs(1, 5)
    for slot in range(4):
        turn_keys(1, slot)
    turn_queries(4)
    turn_queries(5)
    for w in range(2):
        arrived(("p2", w))
        write_keys(mine, w, (kv_own[0, w, 0] + kv_recv[0, w, 0].astype(f32)).astype(bf16))
    write_queries(mine, 0, total_queries(0, 0))

    for half in (4, 5):
        row_dots[half] = normalise(half)
    share(2, 0)

    def gradients(slot):
        for half in (4, 5):
            score_gradients(1, rows(slot), half, row_dots[half])

    def gather_gradients(slot):
        return key_gradients(1, rows(slot), (4, 5))

    gradients(3)
    dk, dv = gather_gradients(3)
    kv_send[1, 0, 0] = dk.astype(bf16)
    start(("s3", 0))
    kv_send[1, 1, 0] = dv.astype(bf16)
    start(("s3", 1))
    gradients(2)
    dk, dv = gather_gradients(2)
    kv_send[1, 0, 2] = dk.astype(bf16)
    start(("s2", 0))
    kv_own[1, 1, 1] = dv
    pass_on(2, 0)
    oq_mate_send[1] = total_queries(1, 1)
    start(("o_m", 1))
    gradients(1)
    gradients(0)
    for half in (4, 5):
        query_gradients(1, half)
    share(2, 1)
    dk, dv = gather_gradients(1)
    kv_send[1, 1, 1] = dv.astype(bf16)
    start(("s1", 1))
    arrived(("s3", 0))
    kv_send[1, 0, 1] = (dk + kv_recv[1, 0, 0].astype(f32)).astype(bf16)
    start(("s1", 0))
    arrived(("s3", 1))
    kv_send[1, 1, 2] = (kv_own[1, 1, 1] + kv_recv[1, 1, 0].astype(f32)).astype(bf16)
    start(("s2", 1))
    dk, dv = gather_gradients(0)
    pass_on(2, 1)
    kv_own[1, 0, 0] = dk
    kv_own[1, 1, 0] = dv

    write_queries(mine, 1, total_queries(0, 1))
    for w in range(2):
        arrived(("p1", w))
        write_keys(theirs, w, kv_recv[0, w, 2])
    for w in range(2):
        arrived(("o_m", w))
        write_queries(theirs, w, oq_mate_recv[w])
    write_queries(1, 0, total_queries(2, 0))
    for w in (1, 0):
        arrived(("s1", w), ("s2", w))
        total = kv_own[1, w, 0] + kv_recv[1, w, 1].astype(f32) + kv_recv[1, w, 2].astype(f32)
        write_keys(1, w, total.astype(bf16))
    write_queries(1, 1, total_queries(2, 1))
    for copy in stores:
        copy.wait()
    for copy in copies.values():
        copy.wait_send()


def hand_over(*refs):
    sources, results, (held, load_sem, store_sem) = refs[:4], refs[4:8], refs[8:]
    loads = [pltpu.make_async_copy(sources[n], held.at[n], load_sem.at[n]) for n in range(4)]
    stores = [pltpu.make_async_copy(held.at[n], results[n], store_sem.at[n]) for n in range(4)]
    for copy in loads:
        copy.start()
    for load, copy in zip(loads, stores):
        load.wait()
        copy.start()
    for copy in stores:
        copy.wait()


def body(queries, key_input, values, cotangent, positions, lengths):
    shape = jax.ShapeDtypeStruct(queries.shape, bf16)
    vmem = pl.BlockSpec(memory_space=pltpu.VMEM)
    hbm = pl.BlockSpec(memory_space=pl.ANY)
    tokens, turned = (TOK, HEAD_DIM), (HEAD_DIM, TOK)
    n = HEADS_DEV
    results = pl.pallas_call(
        kernel,
        out_shape=[shape] * 4,
        in_specs=[hbm] * 4 + [vmem] * 2,
        out_specs=[hbm] * 4,
        scratch_shapes=[
            pltpu.VMEM((4, TOK, HEADS_DEV * HEAD_DIM), bf16),
            pltpu.VMEM((4, TOK, HEADS_DEV * HEAD_DIM), bf16),
            pltpu.SemaphoreType.DMA((4,)),
            pltpu.SemaphoreType.DMA((12,)),
            pltpu.VMEM((n,) + tokens, bf16),
            pltpu.VMEM((n,) + tokens, bf16),
            pltpu.VMEM((n,) + turned, bf16),
            pltpu.VMEM((n,) + turned, bf16),
            pltpu.VMEM((2, ROWS, HEAD_DIM), bf16),
            pltpu.VMEM((2, ROWS, HEAD_DIM), bf16),
            pltpu.VMEM((2, HEAD_DIM, ROWS), bf16),
            pltpu.VMEM((2, HEAD_DIM + 16, ROWS), bf16),
            pltpu.VMEM((HEAD_DIM, QCOLS), bf16),
            pltpu.VMEM((HEAD_DIM, QCOLS), bf16),
            pltpu.VMEM((QCOLS, HEAD_DIM), bf16),
            pltpu.VMEM((QCOLS, HEAD_DIM), bf16),
            pltpu.VMEM((HEAD_DIM, QCOLS), bf16),
            pltpu.VMEM((4, 8, 128), jnp.int32),
            pltpu.VMEM((2, ROWS, HALF), f32),
            pltpu.VMEM((ROWS, 4 * HALF), bf16),
            pltpu.VMEM((ROWS, 4 * HALF), bf16),
            pltpu.VMEM((6, 8, HALF), f32),
            pltpu.VMEM((6, 8, HALF), f32),
            pltpu.VMEM((2, HEAD_DIM, QCOLS), f32),
            pltpu.VMEM((n, 2, 3) + turned, bf16),
            pltpu.VMEM((n, 2, 3) + turned, bf16),
            pltpu.VMEM((2,) + turned, bf16),
            pltpu.VMEM((2,) + turned, bf16),
            pltpu.VMEM((2, 2, 2) + tokens, f32),
            pltpu.VMEM((2, 2, 3) + tokens, bf16),
            pltpu.VMEM((2, 2, 3) + tokens, bf16),
            pltpu.VMEM(turned, f32),
            pltpu.SemaphoreType.DMA((N_SEM,)),
            pltpu.SemaphoreType.DMA((N_SEM,)),
        ],
        compiler_params=pltpu.CompilerParams(
            collective_id=0, has_side_effects=True, vmem_limit_bytes=60 * 1024 * 1024
        ),
        cost_estimate=pl.CostEstimate(
            flops=12 * n * ROWS * ROWS * HEAD_DIM, bytes_accessed=16 << 20, transcendentals=n * ROWS * ROWS
        ),
        name="attention",
    )(queries, key_input, values, cotangent, positions, lengths)
    return pl.pallas_call(
        hand_over,
        out_shape=[shape] * 4,
        in_specs=[hbm] * 4,
        out_specs=[hbm] * 4,
        scratch_shapes=[
            pltpu.VMEM((4, 1, TOK, HEADS_DEV * HEAD_DIM), bf16),
            pltpu.SemaphoreType.DMA((4,)),
            pltpu.SemaphoreType.DMA((4,)),
        ],
        name="hand_over",
    )(*results)


def solution(mesh):
    split = P("tower", "seq", "rep")
    return jax.shard_map(
        body,
        mesh=mesh,
        in_specs=(split, split, split, split, P("tower", "seq"), P("tower", "seq")),
        out_specs=(split, split, split, split),
        check_vma=False,
    )
```

time: 699 us -> 61.5 us (0.09)
  waiting for transfers between devices: 454 us -> 0 us
  local copies, waits for them, and re-layouts: 116 us -> 0 us
  Pallas kernels: 0 us -> 59.4 us
  matrix products: 58.9 us -> 0 us
  other arithmetic: 37.8 us -> 0 us
  blocking collectives: 14.8 us -> 0 us
  between operations: 14.9 us -> 1.47 us
    reduce_scatter x6 -> x0, waiting for transfers between devices: 354 us -> none  [the longest x3 231 us: per_head(): lax.psum_scatter(key_stack, ('tower', 'seq'), scatter_dimension=0, tiled=...]
    all_gather x2 -> x0, waiting for transfers between devices: 99.6 us -> none  [the longest x1 54.3 us: body(): lax.all_gather(value_heads, ('tower', 'seq'), axis=0, tiled=True)]
    pallas_call x0 -> x2, Pallas kernels: none -> 59.4 us  [the longest x1 57.3 us: body(): pl.pallas_call(kernel, out_shape=[shape] * 4, in_specs=[hbm] * 4 + [vmem]...]
    dot_general x36 -> x0, matrix products: 58.9 us -> none  [the longest x6 14.2 us: branch(): jnp.dot(probabilities, value_rows, preferred_element_type=jnp.float32)]
    while x66 -> x0, local copies, waits for them, and re-layouts: 47.7 us -> none
    slice x9 -> x0, local copies, waits for them, and re-layouts: 35 us -> none  [the longest x3 18.3 us: per_head(): value_rows[1]]
    reshape x2 -> x0, local copies, waits for them, and re-layouts: 16.4 us -> none  [the longest x1 8.24 us: body(): val_heads = joined_values.reshape(2, -1, head_count, HEAD_DIM)]
    unnamed x1 -> x0, blocking collectives: 14.8 us -> none
  transfers between devices with their start and end apart: 8 -> 0, of which waited for: 8 -> 0; matrix products, arithmetic and copies ran while one was open for 16% -> 0% of each run, Pallas kernels for 0% -> 0%
where the time goes in v2:
time: 61.5 us; the launch traced here: 60.8 us
  Pallas kernels  59.4 us (97%)
  between operations  1.47 us (2%)
    pallas_call x1, Pallas kernels, body(): pl.pallas_call(kernel, out_shape=[shape] * 4, in_specs=[hbm] * 4 + [vmem]...  57.3 us
    pallas_call x1, Pallas kernels, body(): pl.pallas_call(hand_over, out_shape=[shape] * 4, in_specs=[hbm] * 4, out_...  2.04 us

profile of v2, /device:TPU:0, one launch (start us, length us, event | category | flops | bytes accessed | tf_op | source)
XLA Modules:
  0.0 60.8 jit_solution(12465840059405208468)
XLA Ops:
  1.3 57.3 %attention.1 = (bf16[1,384,384]{2,1,0:T(8,128)(2,1)}, bf16[1,384,384]{2,1,0:T(8,128)(2,1)}, bf16[1,384,384]{2,1,0:T(8,128)(2,1)}, bf16[1,384,384]{2,1,0:T(8,128)(2,1)}) custom-call(bf16[1,384,384]{2,1,0:T(8,128)(2,1)} %q_hbm.1, bf16[1,384,384]{2,1,0:T(8,128)(2,1)} %k_hbm.1, bf16[1,384,384]{2,1,0:T(8,128)(2,1)} %v_hbm.1, bf16[1,384,384]{2,1,0:T(8,128)(2,1)} %g_hbm.1, ...), custom_call_target="tpu_custom_call" | custom-call | flops 10871635968 | bytes 16777216 | tf_op jit(solution)/shard_map/attention/pallas_call | solution.py:494
  58.6 2.0 %hand_over.1 = (bf16[1,384,384]{2,1,0:T(8,128)(2,1)}, bf16[1,384,384]{2,1,0:T(8,128)(2,1)}, bf16[1,384,384]{2,1,0:T(8,128)(2,1)}, bf16[1,384,384]{2,1,0:T(8,128)(2,1)}) custom-call(bf16[1,384,384]{2,1,0:T(8,128)(2,1)} %get-tuple-element.8.refs_0_, bf16[1,384,384]{2,1,0:T(8,128)(2,1)} %get-tuple-element.9.refs_1_, ...), custom_call_target="tpu_custom_call" | custom-call | tf_op jit(solution)/shard_map/hand_over/pallas_call | solution.py:543

commit v3 on v2

--- a/solution.py
+++ b/solution.py
@@ -83,14 +83,16 @@
         for name in names:
             copies[name].wait_recv()
 
-    plan("k_m", khead.at[theirs], kbuf.at[0, rows(1)], mate)
-    plan("v_m", vhead.at[theirs], vbuf.at[0, rows(1)], mate)
+    for n in range(2):
+        part = pl.ds(n * TOK // 2, TOK // 2)
+        first, third = pl.ds(TOK + n * TOK // 2, TOK // 2), pl.ds(3 * TOK + n * TOK // 2, TOK // 2)
+        for name, head, buf in (("k", khead, kbuf), ("v", vhead, vbuf)):
+            plan((name + "_m", n), head.at[theirs, part], buf.at[0, first], mate)
+            plan((name + "_f", n), buf.at[0, first], buf.at[0, third], cross)
     plan("q_m", qhead.at[theirs], qt.at[:, rows(4)], mate)
     plan("g_m", ghead.at[theirs], gt.at[:, rows(4)], mate)
     plan("k_c", khead.at[mine], kbuf.at[0, rows(2)], cross)
     plan("v_c", vhead.at[mine], vbuf.at[0, rows(2)], cross)
-    plan("k_f", kbuf.at[0, rows(1)], kbuf.at[0, rows(3)], cross)
-    plan("v_f", vbuf.at[0, rows(1)], vbuf.at[0, rows(3)], cross)
     plan("k1_m", khead.at[1], kbuf.at[1, rows(1)], mate)
     plan("v1_m", vhead.at[1], vbuf.at[1, rows(1)], mate)
     plan("k1_c", khead.at[1], kbuf.at[1, rows(2)], cross)
@@ -158,7 +160,7 @@
     prepare_keys(0)
     prepare_keys(2)
     pl.semaphore_wait(barrier, 4)
-    start("k_m", "k_c", "l_m", "l_c")
+    start(("k_m", 0), ("k_m", 1), "k_c", "l_m", "l_c")
     kbuf[0, 0:TOK, :] = khead[mine]
     loads["q"].wait()
     loads["g"].wait()
@@ -170,12 +172,10 @@
     loads["v"].wait()
     for h in range(HEADS_DEV):
         vhead[h] = v_in[:, h * HEAD_DIM : (h + 1) * HEAD_DIM]
-    start("v_m", "g_m")
+    start(("v_m", 0), ("v_m", 1), "g_m")
     gt[:, 0:TOK] = ghead[mine]
     start(("g_s", 0), ("g_t", 0))
     vbuf[0, 0:TOK, :] = vhead[mine]
-    arrived("l_m")
-    start("l_f")
 
     def valid_row(slot):
         return (
@@ -221,8 +221,11 @@
         out = dot(vtbuf[st], prob[:, prob_cols(half)])
         oq_own[0, :, cols] = out[0:128, :]
         stat_out[half, 1:2, :] = out[128:129, :]
+
+    def send_stats(half):
+        cols = cols_of(half)
         stat_out[half, 2:3, :] = jnp.sum(
-            out[0:128, :] * gt[:, cols].astype(f32), axis=0, keepdims=True
+            oq_own[0, :, cols] * gt[:, cols].astype(f32), axis=0, keepdims=True
         )
         start(("st", half))
 
@@ -307,81 +310,95 @@
         start(*onward)
 
     def before(slot):
-        if slot == 1:
-            relay("k_m", "k_f", "v_c")
         if slot == 2:
             relay(("q_t", 0), ("q_f", 0))
             arrived("k_c")
         if slot == 3:
             relay("q_m", ("q_s", 1), ("q_t", 1))
-            arrived("k_f")
-
+            arrived(("k_f", 0), ("k_f", 1))
+
+    relay(("k_m", 0), ("k_f", 0))
+    relay(("k_m", 1), ("k_f", 1), "v_c")
+    relay("l_m", "l_f")
     arrived(("q_s", 0))
     scores(0, 0, before)
-    relay("v_m", "v_f")
+    relay(("v_m", 0), ("v_f", 0))
+    relay(("v_m", 1), ("v_f", 1))
     prepare_keys(1)
-    prepare_queries(1)
     kbuf[1, 0:TOK, :] = khead[1]
     vbuf[1, 0:TOK, :] = vhead[1]
+    start("k1_m", "k1_c", "v1_m", "v1_c")
+    arrived(("q_f", 0))
+    scores(0, 1)
+    relay(("g_t", 0), ("g_f", 0))
+    arrived(("q_s", 1))
+    scores(0, 2)
+    relay(("q_t", 1), ("q_f", 1))
+    relay("g_m", ("g_s", 1), ("g_t", 1))
+    prepare_queries(1)
     qt[:, 8 * TOK : 9 * TOK] = qhead[1]
     gt[:, 8 * TOK : 9 * TOK] = ghead[1]
-    start("k1_m", "k1_c", "v1_m", "v1_c")
-    relay(("g_t", 0), ("g_f", 0))
-    arrived(("q_f", 0))
-    scores(0, 1)
-    arrived(("q_s", 1))
-    scores(0, 2)
-    relay("g_m", ("g_s", 1), ("g_t", 1))
-    relay(("q_t", 1), ("q_f", 1))
-    arrived("v_c", "l_c", "l_f", "v_f", ("g_s", 0), ("g_f", 0))
+    start(("q_s", 2), ("q_t", 2), ("g_s", 2), ("g_t", 2))
+    arrived("v_c", "l_c", "l_f", ("v_f", 0), ("v_f", 1))
     for slot in range(4):
         turn_values(0, slot)
     outputs(0, 0)
     outputs(0, 1)
-    start(("q_s", 2), ("q_t", 2), ("g_s", 2), ("g_t", 2))
+    arrived(("g_s", 0), ("g_f", 0))
+    send_stats(0)
+    send_stats(1)
     arrived(("q_f", 1))
     scores(0, 3)
-    arrived(("g_s", 1))
-    outputs(0, 2)
-    relay(("g_t", 1), ("g_f", 1))
     for slot in range(4):
         turn_keys(0, slot)
     for half in range(4):
         turn_queries(half)
+    outputs(0, 2)
+    outputs(0, 3)
+
+    near, far = pl.ds(0, HALF), pl.ds(HALF, HALF)
+    row_dots = [None] * 6
+    for half in (0, 1):
+        row_dots[half] = normalise(half)
+    share(0, 0)
+    for half in (0, 1):
+        score_gradients(0, far, half, row_dots[half])
+    relay(("g_t", 1), ("g_f", 1))
+    arrived(("g_s", 1))
+    send_stats(2)
+    for half in (0, 1):
+        score_gradients(0, near, half, row_dots[half])
     arrived(("g_f", 1))
-    outputs(0, 3)
-
-    row_dots = [None] * 6
-    for v in range(2):
-        for half in (2 * v, 2 * v + 1):
-            row_dots[half] = normalise(half)
-        share(v, 0)
-        for half in (2 * v, 2 * v + 1):
-            score_gradients(0, pl.ds(HALF, HALF), half, row_dots[half])
+    send_stats(3)
+    pass_on(0, 0)
+    for half in (0, 1):
+        query_gradients(0, half)
+    share(0, 1)
     relay("k1_m", "k1_f")
     relay("v1_c", "v1_f")
+    for half in (2, 3):
+        row_dots[half] = normalise(half)
+    share(1, 0)
+    for half in (2, 3):
+        score_gradients(0, far, half, row_dots[half])
+    totals = key_gradients(0, far, (0, 1, 2, 3))
+    for w in range(2):
+        kv_send[0, w, 1] = totals[w][TOK:].astype(bf16)
+        start(("p3", w))
+    for w in range(2):
+        kv_send[0, w, 0] = totals[w][0:TOK].astype(bf16)
+        start(("p2", w))
+    pass_on(1, 0)
     relay(("q_t", 2), ("q_f", 2))
     relay(("g_t", 2), ("g_f", 2))
-    totals = key_gradients(0, pl.ds(HALF, HALF), (0, 1, 2, 3))
-    for w in range(2):
-        kv_send[0, w, 1] = totals[w][TOK:].astype(bf16)
-        start(("p3", w))
-    for w in range(2):
-        kv_send[0, w, 0] = totals[w][0:TOK].astype(bf16)
-        start(("p2", w))
-    pass_on(0, 0)
-    pass_on(1, 0)
-    for half in range(4):
-        score_gradients(0, pl.ds(0, HALF), half, row_dots[half])
+    for half in (2, 3):
+        score_gradients(0, near, half, row_dots[half])
     for half in (2, 3):
         query_gradients(0, half)
     share(1, 1)
-    for half in (0, 1):
-        query_gradients(0, half)
-    share(0, 1)
-    totals = key_gradients(0, pl.ds(0, HALF), (0, 1, 2, 3))
+    pass_on(0, 1)
+    totals = key_gradients(0, near, (0, 1, 2, 3))
     pass_on(1, 1)
-    pass_on(0, 1)
     for w, total in enumerate(totals):
         kv_own[0, w, 0] = total[0:TOK]
         kv_own[0, w, 1] = total[TOK:]
@@ -399,7 +416,9 @@
     for slot in range(4):
         turn_values(1, slot)
     outputs(1, 4)
+    send_stats(4)
     outputs(1, 5)
+    send_stats(5)
     for slot in range(4):
         turn_keys(1, slot)
     turn_queries(4)

time: 61.5 us -> 58.4 us (0.950)
  Pallas kernels: 59.4 us -> 56.8 us
    pallas_call x1, Pallas kernels: 57.3 us -> 54.7 us  [body(): pl.pallas_call(kernel, out_shape=[shape] * 4, in_specs=[hbm] * 4 + [vmem]...]
where the time goes in v3:
time: 58.4 us; the launch traced here: 58.2 us
  Pallas kernels  56.8 us (97%)
  between operations  1.47 us (3%)
    pallas_call x1, Pallas kernels, body(): pl.pallas_call(kernel, out_shape=[shape] * 4, in_specs=[hbm] * 4 + [vmem]...  54.7 us
    pallas_call x1, Pallas kernels, body(): pl.pallas_call(hand_over, out_shape=[shape] * 4, in_specs=[hbm] * 4, out_...  2.04 us

profile of v3, /device:TPU:0, one launch (start us, length us, event | category | flops | bytes accessed | tf_op | source)
XLA Modules:
  0.0 58.2 jit_solution(2799313017655889857)
XLA Ops:
  1.3 54.7 %attention.1 = (bf16[1,384,384]{2,1,0:T(8,128)(2,1)}, bf16[1,384,384]{2,1,0:T(8,128)(2,1)}, bf16[1,384,384]{2,1,0:T(8,128)(2,1)}, bf16[1,384,384]{2,1,0:T(8,128)(2,1)}) custom-call(bf16[1,384,384]{2,1,0:T(8,128)(2,1)} %q_hbm.1, bf16[1,384,384]{2,1,0:T(8,128)(2,1)} %k_hbm.1, bf16[1,384,384]{2,1,0:T(8,128)(2,1)} %v_hbm.1, bf16[1,384,384]{2,1,0:T(8,128)(2,1)} %g_hbm.1, ...), custom_call_target="tpu_custom_call" | custom-call | flops 10871635968 | bytes 16777216 | tf_op jit(solution)/shard_map/attention/pallas_call | solution.py:513
  56.0 2.0 %hand_over.1 = (bf16[1,384,384]{2,1,0:T(8,128)(2,1)}, bf16[1,384,384]{2,1,0:T(8,128)(2,1)}, bf16[1,384,384]{2,1,0:T(8,128)(2,1)}, bf16[1,384,384]{2,1,0:T(8,128)(2,1)}) custom-call(bf16[1,384,384]{2,1,0:T(8,128)(2,1)} %get-tuple-element.8.refs_0_, bf16[1,384,384]{2,1,0:T(8,128)(2,1)} %get-tuple-element.9.refs_1_, ...), custom_call_target="tpu_custom_call" | custom-call | tf_op jit(solution)/shard_map/hand_over/pallas_call | solution.py:562

commit v4 on v3

--- a/solution.py
+++ b/solution.py
@@ -319,11 +319,11 @@
 
     relay(("k_m", 0), ("k_f", 0))
     relay(("k_m", 1), ("k_f", 1), "v_c")
-    relay("l_m", "l_f")
     arrived(("q_s", 0))
     scores(0, 0, before)
     relay(("v_m", 0), ("v_f", 0))
     relay(("v_m", 1), ("v_f", 1))
+    relay("l_m", "l_f")
     prepare_keys(1)
     kbuf[1, 0:TOK, :] = khead[1]
     vbuf[1, 0:TOK, :] = vhead[1]

time: 58.4 us -> 58.5 us (level)
  no operation moved by 1% of the time
where the time goes in v4:
time: 58.5 us; the launch traced here: 58.3 us
  Pallas kernels  56.8 us (97%)
  between operations  1.47 us (3%)
    pallas_call x1, Pallas kernels, body(): pl.pallas_call(kernel, out_shape=[shape] * 4, in_specs=[hbm] * 4 + [vmem]...  54.8 us
    pallas_call x1, Pallas kernels, body(): pl.pallas_call(hand_over, out_shape=[shape] * 4, in_specs=[hbm] * 4, out_...  2.04 us

profile of v4, /device:TPU:0, one launch (start us, length us, event | category | flops | bytes accessed | tf_op | source)
XLA Modules:
  0.0 58.3 jit_solution(17892973956256969948)
XLA Ops:
  1.3 54.8 %attention.1 = (bf16[1,384,384]{2,1,0:T(8,128)(2,1)}, bf16[1,384,384]{2,1,0:T(8,128)(2,1)}, bf16[1,384,384]{2,1,0:T(8,128)(2,1)}, bf16[1,384,384]{2,1,0:T(8,128)(2,1)}) custom-call(bf16[1,384,384]{2,1,0:T(8,128)(2,1)} %q_hbm.1, bf16[1,384,384]{2,1,0:T(8,128)(2,1)} %k_hbm.1, bf16[1,384,384]{2,1,0:T(8,128)(2,1)} %v_hbm.1, bf16[1,384,384]{2,1,0:T(8,128)(2,1)} %g_hbm.1, ...), custom_call_target="tpu_custom_call" | custom-call | flops 10871635968 | bytes 16777216 | tf_op jit(solution)/shard_map/attention/pallas_call | solution.py:513
  56.1 2.0 %hand_over.1 = (bf16[1,384,384]{2,1,0:T(8,128)(2,1)}, bf16[1,384,384]{2,1,0:T(8,128)(2,1)}, bf16[1,384,384]{2,1,0:T(8,128)(2,1)}, bf16[1,384,384]{2,1,0:T(8,128)(2,1)}) custom-call(bf16[1,384,384]{2,1,0:T(8,128)(2,1)} %get-tuple-element.8.refs_0_, bf16[1,384,384]{2,1,0:T(8,128)(2,1)} %get-tuple-element.9.refs_1_, ...), custom_call_target="tpu_custom_call" | custom-call | tf_op jit(solution)/shard_map/hand_over/pallas_call | solution.py:562
